TPU v7x, 128 devices: a whole 4x4x4 slice. The times are simulated.
128 devices in a mesh: shard: 16 (over z, y), ctx: 2 (over x_hi), tp: 4 (over x_lo, core).
Axes of the slice: x: 4 (x_hi: 2, x_lo: 2; x = x_hi * 2 + x_lo), y: 4, z: 4, core: 2. Of those that a mesh axis runs over, the one named last changes fastest.
Arguments:
- hidden_in: bfloat16 [16, 1024, 1024], P('shard', 'ctx'), may hold values from -6 to 6
- w_query: bfloat16 [1024, 1024], P('shard', 'tp'), may hold values from -0.1875 to 0.1875
- key_weight: bfloat16 [1024, 512], P('shard', 'tp'), may hold values from -0.1875 to 0.1875
- value_weight: bfloat16 [1024, 512], P('shard', 'tp'), may hold values from -0.1875 to 0.1875
- w_out: bfloat16 [1024, 1024], P('tp', 'shard'), may hold values from -1.5 to 1.5
- w_gate: bfloat16 [1024, 4608], P('shard', 'tp'), may hold values from -0.1875 to 0.1875
- w_up: bfloat16 [1024, 4608], P('shard', 'tp'), may hold values from -0.1875 to 0.1875
- w_down: bfloat16 [4608, 1024], P('tp', 'shard'), may hold values from -0.09375 to 0.09375
- norm_gains: bfloat16 [2, 1024], P(None, 'shard'), may hold values from 0.099609375 to 1.8984375
- head_gains: bfloat16 [2, 64], P(None, 'shard'), may hold values from 0.099609375 to 1.8984375
- cotangent: bfloat16 [16, 1024, 1024], P('shard', 'ctx'), may hold values from -6 to 6
Outputs:
- block_out: bfloat16 [16, 1024, 1024], P('shard', 'ctx')
- grad_in: float32 [16, 1024, 1024], P('shard', 'ctx')
- grad_w_query: float32 [1024, 1024], P('shard', 'tp')
- grad_w_key: float32 [1024, 512], P('shard', 'tp')
- grad_w_value: float32 [1024, 512], P('shard', 'tp')
- grad_w_out: float32 [1024, 1024], P('tp', 'shard')
- grad_w_gate: float32 [1024, 4608], P('shard', 'tp')
- grad_w_up: float32 [1024, 4608], P('shard', 'tp')
- grad_w_down: float32 [4608, 1024], P('tp', 'shard')
- grad_norm_gains: float32 [2, 1024], P(None, 'shard')
- grad_head_gains: float32 [2, 64], P(None, 'shard')
All inputs are finite; a program needn't handle non-finite values.
Results may differ from a plain program's by a relative error of at most 0.033.
Values may be sent and summed in bfloat16 or wider, within the bound.
A program may use at most 128 MiB of HBM per device.

v0:
```python
import jax
import jax.numpy as jnp
import numpy as np
from jax import lax
from jax.experimental import pallas as pl
from jax.experimental.pallas import tpu as pltpu
from jax.sharding import PartitionSpec as P

HEAD_SIZE = 64
EPS = 1e-05
THETA = 1000000.0
MESH = pl.DeviceIdType.MESH
VMEM_LIMIT = 62 * 1024 * 1024
HALF = 32
QUARTER = 16
SHARD_ROWS = 64


def ring_place():
    me = lax.axis_index("shard")
    return me // 4, lax.rem(me, 4)


def shard_at(z, y):
    return {"shard": lax.rem(z + 4, 4) * 4 + lax.rem(y + 4, 4)}


def greet(partners):
    barrier = pltpu.get_barrier_semaphore()
    for partner in partners:
        pl.semaphore_signal(barrier, inc=1, device_id=partner, device_id_type=MESH)
    pl.semaphore_wait(barrier, len(partners))


def remote(src, dst, send_sem, recv_sem, target):
    return pltpu.make_async_remote_copy(
        src_ref=src,
        dst_ref=dst,
        send_sem=send_sem,
        recv_sem=recv_sem,
        device_id=target,
        device_id_type=MESH,
    )


def torus_partners():
    z, y = ring_place()
    return [shard_at(z, y + 1), shard_at(z, y - 1), shard_at(z + 1, y), shard_at(z - 1, y)]


class Gather:

    def __init__(self, full, columns, send_sem, recv_sem, base):
        self.full = full
        self.columns = columns
        self.send_sem = send_sem
        self.recv_sem = recv_sem
        self.base = base
        self.z, self.y = ring_place()

    def rows(self, half, first, second, part):
        z, y = (self.z + second, self.y + first) if half == 0 else (self.z + first, self.y + second)
        block = lax.rem(z + 4, 4) * 4 + lax.rem(y + 4, 4)
        start = block * SHARD_ROWS + half * HALF + (QUARTER if part == 2 else 0)
        count = HALF if part == 0 else QUARTER
        lo, hi = self.columns
        return self.full.at[pl.ds(pl.multiple_of(start, QUARTER), count), lo:hi]

    def target(self, half, first, second):
        if half == 0:
            return shard_at(self.z + second, self.y + first)
        return shard_at(self.z + first, self.y + second)

    def copy(self, half, k, landed=False):
        if k < 4:
            step = (1, -1)[k % 2]
            if k < 2:
                sent, got = (0, 0, 0), (-step, 0, 0)
            else:
                sent, got = (-step, 0, 1 + k % 2), (-2 * step, 0, 1 + k % 2)
            target = (step, 0)
        else:
            j, kind = (k - 4) // 4, (k - 4) % 4
            offset = (0, -1, 1, 2)[j]
            step = (1, -1)[kind % 2]
            if kind < 2:
                sent, got = (offset, 0, 0), (offset, -step, 0)
            else:
                sent, got = (offset, -step, 1 + kind % 2), (offset, -2 * step, 1 + kind % 2)
            target = (0, step)
        index = self.base + half * 20 + k
        rows = self.rows(half, *(got if landed else sent))
        return remote(
            rows, rows, self.send_sem.at[index], self.recv_sem.at[index], self.target(half, *target)
        )

    def start(self, *ks):
        for k in ks:
            for half in (0, 1):
                self.copy(half, k).start()

    def arrived(self, *ks):
        for k in ks:
            for half in (0, 1):
                self.copy(half, k, True).wait_recv()

    def step(self, n):
        if n == 0:
            self.start(0, 1, 4, 5)
        elif n == 1:
            self.arrived(0)
            self.start(2, 8, 9)
            self.arrived(1)
            self.start(3, 12, 13)
        elif n == 2:
            self.arrived(4)
            self.start(6)
            self.arrived(5)
            self.start(7)
        elif n == 3:
            self.arrived(2, 3)
            self.start(16, 17)
        elif n == 4:
            for k in (8, 9, 12, 13, 16, 17):
                self.arrived(k)
                self.start(k + 2)
        elif n == 5:
            self.arrived(6, 7, 10, 11, 14, 15, 18, 19)

    def finish(self):
        for k in range(20):
            for half in (0, 1):
                self.copy(half, k).wait_send()


class Scatter:

    def __init__(self, part, landing, columns, send_sem, recv_sem, base):
        self.part = part
        self.landing = landing
        self.columns = columns
        self.send_sem = send_sem
        self.recv_sem = recv_sem
        self.base = base
        self.z, self.y = ring_place()

    def place(self, half, first, second):
        if half == 0:
            z, y = self.z + second, self.y + first
        else:
            z, y = self.z + first, self.y + second
        return lax.rem(z + 4, 4) * 4 + lax.rem(y + 4, 4)

    def rows(self, half, first, second, part):
        start = self.place(half, first, second) * SHARD_ROWS + half * HALF
        start = start + (QUARTER if part == 2 else 0)
        count = HALF if part == 0 else QUARTER
        lo, hi = self.columns
        return self.part.at[pl.ds(pl.multiple_of(start, QUARTER), count), lo:hi]

    def slot(self, half, j, kind):
        start = ((half * 5 + j) * 2) * 48 + (kind % 2) * 48 + (QUARTER if kind >= 2 else 0)
        count = HALF if kind >= 2 else QUARTER
        lo, hi = self.columns
        return self.landing.at[start : start + count, lo:hi]

    def copy(self, half, j, kind):
        step = (1, -1)[kind % 2]
        if kind < 2:
            along, part = 2, 1 + kind % 2
        else:
            along, part = step, 0
        if j < 4:
            offset = (2, -1, 1, 0)[j]
            src = self.rows(half, offset, along, part)
            target = {"shard": self.place(half, 0, step)}
        else:
            src = self.rows(half, along, 0, part)
            target = {"shard": self.place(half, step, 0)}
        index = self.base + (half * 5 + j) * 4 + kind
        return remote(src, self.slot(half, j, kind), self.send_sem.at[index], self.recv_sem.at[index], target)

    def add(self, half, target, *slots):
        total = target[...].astype(jnp.float32)
        for slot in slots:
            total = total + slot[...].astype(jnp.float32)
        target[...] = total.astype(jnp.bfloat16)

    def first(self, j):
        for half in (0, 1):
            for kind in (0, 1):
                self.copy(half, j, kind).start()

    def second(self, j):
        for kind in (0, 1):
            for half in (0, 1):
                self.copy(half, j, kind).wait_recv()
                step = (1, -1)[kind]
                if j < 4:
                    target = self.rows(half, (2, -1, 1, 0)[j], step, 1 + kind)
                else:
                    target = self.rows(half, step, 0, 1 + kind)
                self.add(half, target, self.slot(half, j, kind))
                self.copy(half, j, kind + 2).start()

    def third(self, j):
        for half in (0, 1):
            self.copy(half, j, 2).wait_recv()
            self.copy(half, j, 3).wait_recv()
            target = self.rows(half, (2, -1, 1, 0)[j] if j < 4 else 0, 0, 0)
            self.add(half, target, self.slot(half, j, 2), self.slot(half, j, 3))

    def finish(self):
        for half in (0, 1):
            for j in range(5):
                for kind in range(4):
                    self.copy(half, j, kind).wait_send()


def tp_place():
    me = lax.axis_index("tp")
    return me // 2, lax.rem(me, 2)


class TpSum:

    def __init__(self, part, landed, folded, out, send_sem, recv_sem, base):
        self.part, self.landed, self.folded, self.out = part, landed, folded, out
        self.send_sem, self.recv_sem, self.base = send_sem, recv_sem, base
        self.chip, self.core = tp_place()
        self.size = part.shape[0] // 4
        self.mine = self.block(self.chip, self.core)

    def block(self, chip, core):
        return pl.ds(pl.multiple_of((chip * 2 + core) * self.size, self.size), self.size)

    def copy(self, k):
        chip, core = self.chip, self.core
        if k == 0:
            src, dst = self.part.at[self.block(1 - chip, 1 - core)], self.landed.at[0]
        elif k == 1:
            src, dst = self.part.at[self.block(chip, 1 - core)], self.landed.at[1]
        elif k == 2:
            src, dst = self.folded, self.landed.at[2]
        elif k < 5:
            src = dst = self.out.at[self.mine]
        else:
            src = dst = self.out.at[self.block(1 - chip, core)]
        other_core = {"tp": chip * 2 + 1 - core}
        other_chip = {"tp": (1 - chip) * 2 + core}
        target = other_chip if k in (2, 3) else other_core
        return remote(src, dst, self.send_sem.at[self.base + k], self.recv_sem.at[self.base + k], target)

    def begin(self):
        self.copy(0).start()
        self.copy(1).start()

    def fold(self):
        self.copy(0).wait_recv()
        self.folded[...] = (
            self.part[self.block(1 - self.chip, self.core), :].astype(F32) + self.landed[0].astype(F32)
        ).astype(LOW)
        self.copy(2).start()

    def total(self):
        self.copy(1).wait_recv()
        self.copy(2).wait_recv()
        return (
            self.part[self.mine, :].astype(F32)
            + self.landed[1].astype(F32)
            + self.landed[2].astype(F32)
        )

    def back(self):
        self.copy(3).start()
        self.copy(4).start()

    def relay(self):
        self.copy(3).wait_recv()
        self.copy(5).start()

    def end(self):
        self.copy(4).wait_recv()
        self.copy(5).wait_recv()
        for k in range(6):
            self.copy(k).wait_send()


F32 = jnp.float32
LOW = jnp.bfloat16
TOKENS = 512
WIDTH = 1024
ROWS = 256
TILE = 384
TILES = 3
ATTN = 896
STRIDE = 3 * TILE
COLUMNS = ATTN + TILES * STRIDE
CHUNKS = ((0, ATTN),) + tuple((ATTN + STRIDE * t, ATTN + STRIDE * (t + 1)) for t in range(TILES))
SCORE_SCALE = 0.125 * 1.4426950408889634


def dot(left, right, left_dim=1, right_dim=0):
    return lax.dot_general(
        left, right, (((left_dim,), (right_dim,)), ((), ())), preferred_element_type=F32
    )


def iota(shape, dim):
    return lax.broadcasted_iota(jnp.int32, shape, dim)


def row_block(i, size=ROWS):
    return pl.ds(pl.multiple_of(i * size, size), size)


def loop(count, body):
    def step(i, carry):
        body(i)
        return carry

    lax.fori_loop(0, count, step, 0)


def split_dot(value, right):
    high = value.astype(LOW)
    low = (value - high.astype(F32)).astype(LOW)
    return dot(high, right) + dot(low, right)


def swap_halves(value):
    parts = []
    for at in range(0, value.shape[1], 128):
        part = value[:, at : at + 128]
        first = (iota(part.shape, 1) & 32) == 0
        parts.append(jnp.where(first, pltpu.roll(part, 96, 1), pltpu.roll(part, 32, 1)))
    return jnp.concatenate(parts, axis=1)


def wide(table):
    return jnp.concatenate([table, table, table], axis=1)


def to_key_lanes(blocks):
    first = iota(blocks[0].shape, 1) < 64
    zero = jnp.zeros_like(blocks[0])
    return [
        jnp.where(first, blocks[0], zero),
        jnp.where(first, pltpu.roll(blocks[0], 64, 1), zero),
        jnp.where(first, zero, pltpu.roll(blocks[1], 64, 1)),
        jnp.where(first, zero, blocks[1]),
    ]


def from_key_lanes(heads):
    first = iota(heads[0].shape, 1) < 64
    return jnp.concatenate(
        [
            jnp.where(first, heads[0], pltpu.roll(heads[1], 64, 1)),
            jnp.where(first, pltpu.roll(heads[2], 64, 1), heads[3]),
        ],
        axis=1,
    )


def block_kernel(
    hidden_hbm,
    cot_hbm,
    wq,
    wk,
    wv,
    wo,
    wg,
    wu,
    wd,
    norm_gains,
    head_gains,
    table_hbm,
    block_out,
    grad_in,
    out_query,
    out_key,
    out_value,
    out_wo,
    out_norm_gains,
    out_head_gains,
    out_gate,
    out_up,
    out_down,
    hidden,
    cot,
    table,
    w,
    grads,
    landing,
    other,
    normed,
    mlp_in,
    d_branch,
    probs,
    hid,
    dgu,
    q_heads,
    do_heads,
    o_heads,
    kv,
    att,
    attended,
    inverse,
    qk_norm,
    qk_scale,
    d_raw,
    kv_grad,
    kv_send,
    kv_got,
    res_own,
    d_res_own,
    inv_in,
    gain_rows,
    head_gain,
    gain_sums,
    head_mean,
    spread,
    part_a,
    part_b,
    landed,
    folded,
    gain_pass,
    gain_got,
    g_send,
    g_recv,
    s_send,
    s_recv,
    t_send,
    t_recv,
    c_send,
    c_recv,
    l_sem,
):
    me = lax.axis_index("shard")
    ctx = lax.axis_index("ctx")
    chip, core = tp_place()
    own = pl.ds(pl.multiple_of(me * SHARD_ROWS, SHARD_ROWS), SHARD_ROWS)
    ctx_peer = {"ctx": 1 - ctx}
    core_peer = {"tp": chip * 2 + 1 - core}
    chip_peer = {"tp": (1 - chip) * 2 + core}
    later = ctx.astype(F32)

    def weight_copy(k, src, at, count, start=0):
        src = src.at[:, start : start + count]
        return pltpu.make_async_copy(src, w.at[own, at : at + count], l_sem.at[k])

    first_copies = [
        weight_copy(0, wq, 0, 256),
        weight_copy(1, wk, 256, 128),
        weight_copy(2, wv, 384, 128),
        weight_copy(3, wo, 512, 256),
    ]
    tile_copies = [
        weight_copy(4 + 3 * t + k, src, ATTN + STRIDE * t + TILE * k, TILE, TILE * t)
        for t in range(TILES)
        for k, src in enumerate((wg, wu, wd))
    ]
    token_copies = [
        pltpu.make_async_copy(hidden_hbm, hidden, l_sem.at[13]),
        pltpu.make_async_copy(cot_hbm, cot, l_sem.at[14]),
        pltpu.make_async_copy(
            table_hbm.at[pl.ds(pl.multiple_of(ctx * TOKENS, TOKENS), TOKENS)], table, l_sem.at[15]
        ),
    ]
    for copy in first_copies + token_copies[:1] + tile_copies + token_copies[1:]:
        copy.start()
    eye = (iota((64, 64), 0) == iota((64, 64), 1)).astype(F32).astype(LOW)
    gain_sums[...] = jnp.zeros_like(gain_sums)
    gain_sums[0:2, 0:64] = norm_gains[...].astype(F32)
    gain_sums[2:4, 0:4] = head_gains[...].astype(F32)
    row = iota((128, 64), 0)
    block = jnp.zeros((128, 64), F32)
    for k in range(4):
        block = jnp.where(row == k, gain_sums[k : k + 1, 0:64], block)
    w[own, 768:896] = dot(eye, block.astype(LOW), 1, 1).astype(LOW)
    greet(torus_partners() + [ctx_peer, core_peer, chip_peer])
    gather = [Gather(w, chunk, g_send, g_recv, 40 * i) for i, chunk in enumerate(CHUNKS)]
    scatter = [Scatter(grads, landing, chunk, s_send, s_recv, 40 * i) for i, chunk in enumerate(CHUNKS)]
    for copy in first_copies:
        copy.wait()
    gather[0].step(0)

    head_mean[...] = jnp.where(
        (iota((384, 384), 0) // 64) == (iota((384, 384), 1) // 64), 1.0 / 64, 0.0
    ).astype(LOW)
    deep, lane = iota((WIDTH, 128), 0), iota((WIDTH, 128), 1)
    spread[...] = jnp.where(
        jnp.logical_and(deep % 64 < 4, (deep // 64) * 4 + deep % 64 == lane % 64), 1.0, 0.0
    ).astype(LOW)
    gain_sums[...] = jnp.zeros_like(gain_sums)
    kv[:, 256:384] = jnp.ones((2 * TOKENS, 128), LOW)
    for copy in tile_copies + token_copies:
        copy.wait()
    gather[0].step(1)

    def input_scale(i):
        x = hidden[row_block(i), :].astype(F32)
        inv_in[row_block(i), :] = lax.rsqrt(jnp.mean(x * x, axis=1, keepdims=True) + EPS)

    loop(2, input_scale)
    gather[0].step(2)
    gather[1].step(0)
    gather[0].step(3)
    gather[0].step(4)
    gather[0].step(5)
    gather[2].step(0)
    gather[1].step(1)

    pick = (iota((16, 128), 0) == iota((16, 128), 1)).astype(F32).astype(LOW)
    gain_rows[...] = dot(pick, w[:, 768:896], 1, 1)
    head_rows = dot(gain_rows[...].astype(LOW), spread[...])
    head_gain[...] = jnp.concatenate([head_rows[2:3], head_rows[2:3], head_rows[3:4]], axis=1)

    def angles(rows):
        return wide(table[rows, 0:128]), wide(table[rows, 128:256])

    def project(i):
        rows = row_block(i)
        x = hidden[rows, :].astype(F32) * inv_in[rows, :]
        low = (x * gain_rows[0:1, :]).astype(LOW)
        normed[rows, :] = low
        raw = dot(low, w[:, 0:512])
        qk = raw[:, 0:384]
        scale = lax.rsqrt(split_dot(qk * qk, head_mean[...]) + EPS)
        unit = qk * scale
        qk_norm[rows, :] = unit
        qk_scale[rows, :] = scale
        unit = unit * head_gain[...]
        cos, sin = angles(rows)
        turned = unit * cos + swap_halves(unit) * sin
        for h, head in enumerate(to_key_lanes([turned[:, 0:128], turned[:, 128:256]])):
            q_heads[h, rows, :] = head.astype(LOW)
        mine = pl.ds(pl.multiple_of(TOKENS + i * ROWS, ROWS), ROWS)
        kv[mine, 0:128] = turned[:, 256:384].astype(LOW)
        kv[mine, 128:256] = raw[:, 384:512].astype(LOW)

    loop(2, project)
    kv_copy = remote(
        kv.at[TOKENS : 2 * TOKENS, 0:256],
        kv.at[0:TOKENS, 0:256],
        c_send.at[0],
        c_recv.at[0],
        ctx_peer,
    )
    kv_copy.start()
    gather[1].step(2)
    gather[3].step(0)

    def attend_own(h):
        for i in range(2):
            rows, count = slice(ROWS * i, ROWS * (i + 1)), ROWS * (i + 1)
            keys = slice(TOKENS, TOKENS + count)
            scores = dot(q_heads[h, rows, :], kv[keys, 0:128], 1, 1)
            seen = iota(scores.shape, 1) <= iota(scores.shape, 0) + ROWS * i
            weights = jnp.where(seen, jnp.exp2(scores * SCORE_SCALE), 0.0).astype(LOW)
            probs[h, rows, keys] = weights
            o_heads[h, rows, :] = dot(weights, kv[keys, 128:384])

    def attend_other(h):
        for i in range(2):
            rows, keys = slice(ROWS * i, ROWS * (i + 1)), slice(0, TOKENS)
            scores = dot(q_heads[h, rows, :], kv[keys, 0:128], 1, 1)
            weights = (jnp.exp2(scores * SCORE_SCALE) * later).astype(LOW)
            probs[h, rows, keys] = weights
            o_heads[h, rows, :] += dot(weights, kv[keys, 128:384])

    loop(4, attend_own)
    gather[1].step(3)
    gather[2].step(1)
    kv_copy.wait()
    loop(4, attend_other)
    gather[1].step(4)
    gather[2].step(2)

    sums = [
        TpSum(part, landed.at[k], folded.at[k % 2], out, t_send, t_recv, 6 * k)
        for k, (part, out) in enumerate(
            ((part_a, mlp_in), (part_b, d_branch), (part_a, block_out), (part_b, grad_in))
        )
    ]
    mine = sums[0].mine

    def attended_rows(i):
        rows = row_block(i, 128)
        values = [o_heads[h, rows, :] for h in range(4)]
        scale = [1.0 / value[:, 128:256] for value in values]
        heads = from_key_lanes([value[:, 0:128] * s for value, s in zip(values, scale)])
        first = iota((128, 128), 1) < 64
        inverse[rows, :] = jnp.concatenate(
            [jnp.where(first, scale[0], scale[1]), jnp.where(first, scale[2], scale[3])], axis=1
        )
        att[rows, :] = heads
        attended[rows, :] = heads.astype(LOW)
        part_a[rows, :] = dot(heads.astype(LOW), w[:, 512:768], 1, 1).astype(LOW)

    loop(4, attended_rows)
    sums[0].begin()
    gather[1].step(5)
    sums[0].fold()
    gather[2].step(3)
    gather[3].step(1)
    residual = hidden[mine, :].astype(F32) + sums[0].total()
    res_scale = lax.rsqrt(jnp.mean(residual * residual, axis=1, keepdims=True) + EPS)
    res_own[...] = residual
    mlp_in[mine, :] = (residual * res_scale * gain_rows[1:2, :]).astype(LOW)
    sums[0].back()
    gather[2].step(4)
    gather[3].step(2)
    sums[0].relay()
    gather[3].step(3)
    sums[0].end()

    for t in range(TILES):
        at = ATTN + STRIDE * t
        if t == 1:
            gather[2].step(5)
            gather[3].step(4)
        if t == 2:
            gather[3].step(5)

        def feed(i):
            rows = row_block(i)
            both = dot(mlp_in[rows, :], w[:, at : at + 2 * TILE])
            gate, up = both[:, 0:TILE], both[:, TILE : 2 * TILE]
            sigma = jax.nn.sigmoid(gate)
            silu = gate * sigma
            hid[t, rows, :] = (silu * up).astype(LOW)
            d_hidden = dot(cot[rows, :], w[:, at + 2 * TILE : at + 3 * TILE])
            d_gate = d_hidden * up * sigma * (1.0 + gate * (1.0 - sigma))
            dgu[t, rows, 0:TILE] = d_gate.astype(LOW)
            dgu[t, rows, TILE : 2 * TILE] = (d_hidden * silu).astype(LOW)

        loop(2, feed)

    def mlp_back(n):
        rows = row_block(n)
        total = None
        for t in range(TILES):
            at = ATTN + STRIDE * t
            term = dot(dgu[t], w[rows, at : at + 2 * TILE], 1, 1)
            total = term if total is None else total + term
        part_b[:, rows] = total.astype(LOW)

    def mlp_out(n):
        rows = row_block(n)
        total = None
        for t in range(TILES):
            at = ATTN + STRIDE * t + 2 * TILE
            term = dot(hid[t], w[rows, at : at + TILE], 1, 1)
            total = term if total is None else total + term
        part_a[:, rows] = total.astype(LOW)

    def weight_grads(t):
        at = ATTN + STRIDE * t

        def rows_of(n):
            rows = row_block(n)
            grads[rows, at : at + 2 * TILE] = dot(mlp_in[:, rows], dgu[t], 0, 0).astype(LOW)
            grads[rows, at + 2 * TILE : at + 3 * TILE] = dot(cot[:, rows], hid[t], 0, 0).astype(LOW)

        loop(4, rows_of)
        for j in range(4):
            scatter[t + 1].first(j)

    loop(4, mlp_back)
    sums[1].begin()
    weight_grads(0)
    sums[1].fold()
    loop(4, mlp_out)
    sums[2].begin()
    weight_grads(1)
    residual = res_own[...]
    res_scale = lax.rsqrt(jnp.mean(residual * residual, axis=1, keepdims=True) + EPS)
    unit = residual * res_scale
    d_mlp_in = sums[1].total()
    gain_sums[1:2, :] = jnp.sum(d_mlp_in * unit, axis=0, keepdims=True)
    d_unit = d_mlp_in * gain_rows[1:2, :]
    d_res = cot[mine, :].astype(F32) + res_scale * (
        d_unit - unit * jnp.mean(d_unit * unit, axis=1, keepdims=True)
    )
    d_res_own[...] = d_res
    d_branch[mine, :] = d_res.astype(LOW)
    sums[1].back()
    sums[2].fold()
    weight_grads(2)
    sums[1].relay()
    for j in range(4):
        scatter[1].second(j)
    sums[1].end()
    block_out[mine, :] = (res_own[...] + sums[2].total()).astype(LOW)
    sums[2].back()

    def attended_back(i):
        rows = row_block(i)
        d_att = dot(d_branch[rows, :], w[:, 512:768]).astype(LOW).astype(F32)
        scaled = (d_att * inverse[rows, :]).astype(LOW).astype(F32)
        delta = -split_dot(scaled * att[rows, :], head_mean[0:256, 0:256])
        first = iota((ROWS, 128), 1) < 64
        moved = to_key_lanes([scaled[:, 0:128], scaled[:, 128:256]])
        for h in range(4):
            part = delta[:, 128 * (h // 2) : 128 * (h // 2 + 1)]
            high = part.astype(LOW).astype(F32)
            rest = pltpu.roll(part - high, 64, 1)
            do_heads[h, rows, 0:128] = moved[h].astype(LOW)
            do_heads[h, rows, 128:256] = (
                jnp.where(first, high, rest) if h % 2 == 0 else jnp.where(first, rest, high)
            ).astype(LOW)

    loop(2, attended_back)
    kv_grad[...] = jnp.zeros_like(kv_grad)

    def back_piece(h, rows, keys):
        weights = probs[h, rows, keys]
        d_probs = dot(do_heads[h, rows, :], kv[keys, 128:384], 1, 1)
        d_scores = (weights.astype(F32) * d_probs).astype(LOW)
        kv_grad[keys, 0:128] += dot(d_scores, q_heads[h, rows, :], 0, 0)
        kv_grad[keys, 128:256] += dot(weights, do_heads[h, rows, 0:128], 0, 0)
        return dot(d_scores, kv[keys, 0:128])

    def back_other(h):
        for i in range(2):
            rows = slice(ROWS * i, ROWS * (i + 1))
            o_heads[h, rows, 0:128] = back_piece(h, rows, slice(0, TOKENS))

    def back_own(h):
        for i in range(2):
            rows = slice(ROWS * i, ROWS * (i + 1))
            o_heads[h, rows, 0:128] += back_piece(h, rows, slice(TOKENS, TOKENS + ROWS * (i + 1)))

    loop(4, back_other)
    kv_send[:, 0:128] = (kv_grad[0:TOKENS, 0:128] * 0.125).astype(LOW)
    kv_send[:, 128:256] = kv_grad[0:TOKENS, 128:256].astype(LOW)
    kv_back = remote(kv_send, kv_got, c_send.at[1], c_recv.at[1], ctx_peer)
    kv_back.start()
    sums[2].relay()
    for j in range(4):
        scatter[2].second(j)
    for j in range(3):
        scatter[1].third(j)
    scatter[1].first(4)
    scatter[1].third(3)
    loop(4, back_own)
    for j in range(4):
        scatter[3].second(j)
    for j in range(3):
        scatter[2].third(j)
    scatter[2].first(4)
    scatter[2].third(3)
    scatter[1].second(4)
    sums[2].end()
    kv_back.wait()

    def raw_back(i):
        rows = row_block(i)
        dq = from_key_lanes([o_heads[h, rows, 0:128] for h in range(4)]) * 0.125
        mine_rows = pl.ds(pl.multiple_of(TOKENS + i * ROWS, ROWS), ROWS)
        got = kv_got[rows, :].astype(F32)
        dk = kv_grad[mine_rows, 0:128] * 0.125 + got[:, 0:128]
        d_raw[rows, 384:512] = (kv_grad[mine_rows, 128:256] + got[:, 128:256]).astype(LOW)
        turned = jnp.concatenate([dq, dk], axis=1).astype(LOW).astype(F32)
        cos, sin = angles(rows)
        d_out = turned * cos - swap_halves(turned) * sin
        unit = qk_norm[rows, :]
        gain_sums[4:5, 0:384] += jnp.sum(d_out * unit, axis=0, keepdims=True)
        d_unit = d_out * head_gain[...]
        inner = split_dot(d_unit * unit, head_mean[...])
        d_raw[rows, 0:384] = (qk_scale[rows, :] * (d_unit - unit * inner)).astype(LOW)

    loop(2, raw_back)

    def normed_back(i):
        rows = row_block(i)
        d_normed = dot(d_raw[rows, :], w[:, 0:512], 1, 1)
        unit = hidden[rows, :].astype(F32) * inv_in[rows, :]
        gain_sums[0:1, :] += jnp.sum(d_normed * unit, axis=0, keepdims=True)
        part_b[rows, :] = d_normed.astype(LOW)

    loop(2, normed_back)
    sums[3].begin()

    def attention_grads(n):
        rows = row_block(n)
        grads[rows, 0:512] = dot(normed[:, rows], d_raw[...], 0, 0).astype(LOW)
        grads[rows, 512:768] = dot(d_branch[:, rows], attended[...], 0, 0).astype(LOW)

    loop(4, attention_grads)
    heads = gain_sums[4:5, 0:384]
    head_row = iota((16, 128), 0)
    head_sums = jnp.where(
        head_row == 2,
        heads[:, 0:128] + heads[:, 128:256],
        jnp.where(head_row == 3, heads[:, 256:384], 0.0),
    )
    row = iota((16, WIDTH), 0)
    gain_all = jnp.where(
        row == 0,
        gain_sums[0:1, :],
        jnp.where(row == 1, gain_sums[1:2, :], dot(head_sums.astype(LOW), spread[...], 1, 1)),
    )
    grads[:, 768:896] = dot(gain_all.astype(LOW), pick, 0, 0).astype(LOW)
    for j in range(4):
        scatter[0].first(j)
    sums[3].fold()

    def swap_chunk(i):
        lo, hi = CHUNKS[i] if i else (0, 768)
        return remote(
            grads.at[own, lo:hi], other.at[:, lo:hi], c_send.at[2 + i], c_recv.at[2 + i], ctx_peer
        )

    for j in range(3):
        scatter[3].third(j)
    scatter[3].first(4)
    scatter[3].third(3)
    scatter[1].third(4)
    swap_chunk(1).start()
    scatter[2].second(4)
    for j in range(4):
        scatter[0].second(j)
    d_normed = sums[3].total()
    unit = hidden[mine, :].astype(F32) * inv_in[mine, :]
    d_unit = d_normed * gain_rows[0:1, :]
    grad_in[mine, :] = (
        d_res_own[...]
        + inv_in[mine, :] * (d_unit - unit * jnp.mean(d_unit * unit, axis=1, keepdims=True))
    ).astype(LOW)
    sums[3].back()
    for j in range(3):
        scatter[0].third(j)
    scatter[0].first(4)
    scatter[0].third(3)
    scatter[2].third(4)
    swap_chunk(2).start()
    scatter[3].second(4)
    scatter[0].second(4)
    sums[3].relay()
    scatter[3].third(4)
    swap_chunk(3).start()
    scatter[0].third(4)
    swap_chunk(0).start()

    def gain_copy(k, src, target):
        return remote(src, gain_got.at[k], c_send.at[6 + k], c_recv.at[6 + k], target)

    gain_pass[0] = grads[own, 768:896]
    passes = [
        gain_copy(k, gain_pass.at[k], target)
        for k, target in enumerate((core_peer, chip_peer, ctx_peer))
    ]
    for k in range(3):
        passes[k].start()
        passes[k].wait()
        if k < 2:
            total = gain_pass[k].astype(F32) + gain_got[k].astype(F32)
            gain_pass[k + 1] = total.astype(LOW)
        else:
            turned = dot(pick, gain_pass[k], 1, 1) + dot(pick, gain_got[k], 1, 1)
            out_norm_gains[...] = turned[0:2, :]
            out_head_gains[...] = turned[2:4, 0:4]

    def both_sums(lo, hi):
        return grads[own, lo:hi].astype(F32) + other[:, lo:hi].astype(F32)

    for t in range(TILES):
        swap_chunk(t + 1).wait()
        at, lanes = ATTN + STRIDE * t, slice(TILE * t, TILE * (t + 1))
        out_gate[:, lanes] = both_sums(at, at + TILE)
        out_up[:, lanes] = both_sums(at + TILE, at + 2 * TILE)
        out_down[:, lanes] = both_sums(at + 2 * TILE, at + 3 * TILE)
    swap_chunk(0).wait()
    out_query[...] = both_sums(0, 256)
    out_key[...] = both_sums(256, 384)
    out_value[...] = both_sums(384, 512)
    out_wo[...] = both_sums(512, 768)
    sums[3].end()
    for chunk in gather:
        chunk.finish()
    for chunk in scatter:
        chunk.finish()


def rotation_tables():
    frequency = THETA ** (-np.arange(32) / 32.0)
    angles = np.arange(2 * TOKENS)[:, None] * frequency[None, :]
    cosine, sine = np.cos(angles), np.sin(angles)
    return np.concatenate([cosine] * 4 + [-sine, sine] * 2, axis=1).astype(np.float32)


def per_device(
    hidden_in,
    w_query,
    key_weight,
    value_weight,
    w_out,
    w_gate,
    w_up,
    w_down,
    norm_gains,
    head_gains,
    cotangent,
):
    vmem = pl.BlockSpec(memory_space=pltpu.VMEM)
    hbm = pl.BlockSpec(memory_space=pl.ANY)

    def out(shape, dtype):
        return jax.ShapeDtypeStruct(shape, dtype)

    outs = [
        out((TOKENS, WIDTH), LOW),
        out((TOKENS, WIDTH), LOW),
        out((SHARD_ROWS, 256), F32),
        out((SHARD_ROWS, 128), F32),
        out((SHARD_ROWS, 128), F32),
        out((SHARD_ROWS, 256), F32),
        out((2, SHARD_ROWS), F32),
        out((2, 4), F32),
        out((SHARD_ROWS, TILE * TILES), F32),
        out((SHARD_ROWS, TILE * TILES), F32),
        out((SHARD_ROWS, TILE * TILES), F32),
    ]
    scratch = [
        pltpu.VMEM((TOKENS, WIDTH), LOW),
        pltpu.VMEM((TOKENS, WIDTH), LOW),
        pltpu.VMEM((TOKENS, 256), F32),
        pltpu.VMEM((WIDTH, COLUMNS), LOW),
        pltpu.VMEM((WIDTH, COLUMNS), LOW),
        pltpu.VMEM((960, COLUMNS), LOW),
        pltpu.VMEM((SHARD_ROWS, COLUMNS), LOW),
        pltpu.VMEM((TOKENS, WIDTH), LOW),
        pltpu.VMEM((TOKENS, WIDTH), LOW),
        pltpu.VMEM((TOKENS, WIDTH), LOW),
        pltpu.VMEM((4, TOKENS, 2 * TOKENS), LOW),
        pltpu.VMEM((TILES, TOKENS, TILE), LOW),
        pltpu.VMEM((TILES, TOKENS, 2 * TILE), LOW),
        pltpu.VMEM((4, TOKENS, 128), LOW),
        pltpu.VMEM((4, TOKENS, 256), LOW),
        pltpu.VMEM((4, TOKENS, 256), F32),
        pltpu.VMEM((2 * TOKENS, 384), LOW),
        pltpu.VMEM((TOKENS, 256), F32),
        pltpu.VMEM((TOKENS, 256), LOW),
        pltpu.VMEM((TOKENS, 256), F32),
        pltpu.VMEM((TOKENS, 384), F32),
        pltpu.VMEM((TOKENS, 384), F32),
        pltpu.VMEM((TOKENS, 512), LOW),
        pltpu.VMEM((2 * TOKENS, 256), F32),
        pltpu.VMEM((TOKENS, 256), LOW),
        pltpu.VMEM((TOKENS, 256), LOW),
        pltpu.VMEM((TOKENS // 4, WIDTH), F32),
        pltpu.VMEM((TOKENS // 4, WIDTH), F32),
        pltpu.VMEM((TOKENS, 1), F32),
        pltpu.VMEM((16, WIDTH), F32),
        pltpu.VMEM((1, 384), F32),
        pltpu.VMEM((8, WIDTH), F32),
        pltpu.VMEM((384, 384), LOW),
        pltpu.VMEM((WIDTH, 128), LOW),
        pltpu.VMEM((TOKENS, WIDTH), LOW),
        pltpu.VMEM((TOKENS, WIDTH), LOW),
        pltpu.VMEM((4, 3, TOKENS // 4, WIDTH), LOW),
        pltpu.VMEM((2, TOKENS // 4, WIDTH), LOW),
        pltpu.VMEM((3, SHARD_ROWS, 128), LOW),
        pltpu.VMEM((3, SHARD_ROWS, 128), LOW),
        pltpu.SemaphoreType.DMA((160,)),
        pltpu.SemaphoreType.DMA((160,)),
        pltpu.SemaphoreType.DMA((160,)),
        pltpu.SemaphoreType.DMA((160,)),
        pltpu.SemaphoreType.DMA((24,)),
        pltpu.SemaphoreType.DMA((24,)),
        pltpu.SemaphoreType.DMA((9,)),
        pltpu.SemaphoreType.DMA((9,)),
        pltpu.SemaphoreType.DMA((16,)),
    ]
    (
        block_out,
        grad_in,
        r_query,
        r_key,
        r_value,
        r_out,
        r_norm_gains,
        r_head_gains,
        r_gate,
        r_up,
        r_down,
    ) = pl.pallas_call(
        block_kernel,
        out_shape=outs,
        in_specs=[hbm] * 9 + [vmem] * 2 + [hbm],
        out_specs=[vmem] * 11,
        scratch_shapes=scratch,
        compiler_params=pltpu.CompilerParams(
            collective_id=0, has_side_effects=True, vmem_limit_bytes=VMEM_LIMIT
        ),
        name="transformer_block",
    )(
        hidden_in[0],
        cotangent[0],
        w_query,
        key_weight,
        value_weight,
        w_out.T,
        w_gate,
        w_up,
        w_down.T,
        norm_gains,
        head_gains,
        rotation_tables(),
    )
    return (
        block_out[None],
        grad_in.astype(F32)[None],
        r_query,
        r_key,
        r_value,
        r_out.T,
        r_gate,
        r_up,
        r_down.T,
        r_norm_gains,
        r_head_gains,
    )


def solution(mesh):
    placed = (
        P("shard", "ctx", None),
        P("shard", "tp"),
        P("shard", "tp"),
        P("shard", "tp"),
        P("tp", "shard"),
        P("shard", "tp"),
        P("shard", "tp"),
        P("tp", "shard"),
        P(None, "shard"),
        P(None, "shard"),
        P("shard", "ctx", None),
    )
    return jax.shard_map(
        per_device,
        mesh=mesh,
        in_specs=placed,
        out_specs=(
            P("shard", "ctx", None),
            P("shard", "ctx", None),
            P("shard", "tp"),
            P("shard", "tp"),
            P("shard", "tp"),
            P("tp", "shard"),
            P("shard", "tp"),
            P("shard", "tp"),
            P("tp", "shard"),
            P(None, "shard"),
            P(None, "shard"),
        ),
        check_vma=False,
    )
```

profile of v0, /device:TPU:1, one launch (start us, length us, event | category | flops | bytes accessed | tf_op | source)
XLA Modules:
  0.0 160.6 jit_solution(1746682552487633799)
XLA Ops:
  0.6 150.2 %transformer_block.1 = (bf16[512,1024]{1,0:T(8,128)(2,1)}, bf16[512,1024]{1,0:T(8,128)(2,1)}, f32[64,256]{1,0:T(8,128)}, f32[64,128]{1,0:T(8,128)}, f32[64,128]{...) custom-call(bf16[512,1024]{1,0:T(8,128)(2,1)} %bitcast.11, ...), custom_call_target="tpu_custom_call" | custom-call | tf_op jit(solution)/shard_map/transformer_block/pallas_call | solution.py:990
  150.8 0.0 copy-start
  150.8 0.0 copy-start.5
  150.8 0.0 copy-start.7
  150.9 0.0 copy-start.6
  150.9 0.0 copy-start.4
  150.9 0.0 copy-start.3
  150.9 2.9 %bitcast_convert_fusion = f32[1,512,1024]{2,1,0:T(8,128)} fusion(bf16[512,1024]{1,0:T(8,128)(2,1)} %get-tuple-element.23), kind=kLoop, calls=%fused_computation | loop fusion | flops 524288 | bytes 3145728 | tf_op jit(solution)/shard_map/broadcast_in_dim | solution.py:1016
  153.8 0.0 copy-done
  153.8 0.0 copy-start.2
  153.8 0.0 copy-start.1
  153.8 0.0 copy-start.9
  153.8 0.0 copy-start.8
  153.8 1.0 copy.33
  154.8 0.0 copy-done.5
  154.8 0.6 copy.34
  155.4 0.0 copy-done.7
  155.4 0.6 copy.35
  156.0 0.0 copy-done.6
  156.0 0.6 copy.36
  156.6 0.0 copy-done.4
  156.6 0.6 copy.37
  157.3 0.0 copy-done.3
  157.3 0.7 copy.38
  158.0 0.0 copy-done.2
  158.0 0.7 copy.39
  158.7 0.0 copy-done.1
  158.7 0.7 copy.40
  159.4 0.0 copy-done.9
  159.4 0.6 copy.41
  160.0 0.0 copy-done.8
  160.0 0.6 copy.42
Async XLA Ops:
  150.8 3.0 %copy-start = (bf16[512,1024]{1,0:T(8,128)(2,1)S(1)}, bf16[512,1024]{1,0:T(8,128)(2,1)}, u32[]{:S(2)}) copy-start(bf16[512,1024]{1,0:T(8,128)(2,1)} %get-tuple-element.22) | copy-start | bytes 3145732
  150.8 3.9 %copy-start.5 = (f32[64,256]{1,0:T(8,128)S(1)}, f32[64,256]{1,0:T(8,128)}, u32[]{:S(2)}) copy-start(f32[64,256]{1,0:T(8,128)} %get-tuple-element.46) | copy-start | bytes 196612
  150.8 4.6 %copy-start.7 = (f32[64,128]{1,0:T(8,128)S(1)}, f32[64,128]{1,0:T(8,128)}, u32[]{:S(2)}) copy-start(f32[64,128]{1,0:T(8,128)} %get-tuple-element.47) | copy-start | bytes 98308
  150.9 5.2 %copy-start.6 = (f32[64,128]{1,0:T(8,128)S(1)}, f32[64,128]{1,0:T(8,128)}, u32[]{:S(2)}) copy-start(f32[64,128]{1,0:T(8,128)} %get-tuple-element.48) | copy-start | bytes 98308
  150.9 5.8 %copy-start.4 = (f32[64,256]{1,0:T(8,128)S(1)}, f32[64,256]{1,0:T(8,128)}, u32[]{:S(2)}) copy-start(f32[64,256]{1,0:T(8,128)} %get-tuple-element.27) | copy-start | bytes 196612
  150.9 6.4 %copy-start.3 = (f32[64,1152]{1,0:T(8,128)S(1)}, f32[64,1152]{1,0:T(8,128)}, u32[]{:S(2)}) copy-start(f32[64,1152]{1,0:T(8,128)} %get-tuple-element.50) | copy-start | bytes 884740
  153.8 4.2 %copy-start.2 = (f32[64,1152]{1,0:T(8,128)S(1)}, f32[64,1152]{1,0:T(8,128)}, u32[]{:S(2)}) copy-start(f32[64,1152]{1,0:T(8,128)} %get-tuple-element.51) | copy-start | bytes 884740
  153.8 4.9 %copy-start.1 = (f32[64,1152]{1,0:T(8,128)S(1)}, f32[64,1152]{1,0:T(8,128)}, u32[]{:S(2)}) copy-start(f32[64,1152]{1,0:T(8,128)} %get-tuple-element.30) | copy-start | bytes 884740
  153.8 5.6 %copy-start.9 = (f32[2,64]{1,0:T(2,128)S(1)}, f32[2,64]{1,0:T(2,128)}, u32[]{:S(2)}) copy-start(f32[2,64]{1,0:T(2,128)} %get-tuple-element.53) | copy-start | bytes 1540
  153.8 6.2 %copy-start.8 = (f32[2,4]{1,0:T(2,128)S(1)}, f32[2,4]{1,0:T(2,128)}, u32[]{:S(2)}) copy-start(f32[2,4]{1,0:T(2,128)} %get-tuple-element.54) | copy-start | bytes 100
where the time goes:
time: 162 us; the launch traced here: 161 us
  Pallas kernels  150 us (93%)
  local copies, waits for them, and re-layouts  6.77 us (4%)
  other arithmetic  2.89 us (2%)
    pallas_call x1, Pallas kernels, per_device(): pl.pallas_call(block_kernel, out_shape=outs, in_specs=[hbm] * 9 + [vmem]...  150 us
    unnamed x30, local copies, waits for them, and re-layouts  6.77 us

commit v1 on v0

--- a/solution.py
+++ b/solution.py
@@ -224,15 +224,17 @@
 
 class TpSum:
 
-    def __init__(self, part, landed, folded, out, send_sem, recv_sem, base):
+    def __init__(self, half, part, landed, folded, out, send_sem, recv_sem, base):
+        self.half = half
         self.part, self.landed, self.folded, self.out = part, landed, folded, out
         self.send_sem, self.recv_sem, self.base = send_sem, recv_sem, base
         self.chip, self.core = tp_place()
-        self.size = part.shape[0] // 4
         self.mine = self.block(self.chip, self.core)
+        self.local = slice(half * SHARE, (half + 1) * SHARE)
 
     def block(self, chip, core):
-        return pl.ds(pl.multiple_of((chip * 2 + core) * self.size, self.size), self.size)
+        start = (chip * 2 + core) * 2 * SHARE + self.half * SHARE
+        return pl.ds(pl.multiple_of(start, SHARE), SHARE)
 
     def copy(self, k):
         chip, core = self.chip, self.core
@@ -291,12 +293,38 @@
 TOKENS = 512
 WIDTH = 1024
 ROWS = 256
+SHARE = 64
 TILE = 384
 TILES = 3
 ATTN = 896
+GAINS = 512
+OUT = 640
 STRIDE = 3 * TILE
 COLUMNS = ATTN + TILES * STRIDE
 CHUNKS = ((0, ATTN),) + tuple((ATTN + STRIDE * t, ATTN + STRIDE * (t + 1)) for t in range(TILES))
+PARTS = ((0, OUT),) + tuple(
+    (ATTN + STRIDE * t, ATTN + STRIDE * (t + 1)) for t in range(TILES)
+) + ((OUT, ATTN),)
+POLLS = {
+    "scale": ((0, 2), (1, 0), (0, 3), (0, 4), (0, 5), (1, 1), (2, 0)),
+    "own3": ((1, 2), (1, 3), (2, 1), (3, 0)),
+    "fold": ((1, 4), (2, 2), (2, 3), (3, 1)),
+    "back": ((1, 5), (2, 4), (3, 2), (3, 3)),
+    "tile1": ((2, 5), (3, 4)),
+    "tile2": ((3, 5),),
+}
+SUMS = {
+    "begin1": ((1, 0),),
+    "fold1": ((2, 0),),
+    "grads": ((3, 0),),
+    "back1": ((1, 1),),
+    "outgrads": ((4, 0),),
+    "other": ((2, 1),),
+    "block": ((1, 2), (3, 1), (2, 2), (4, 1),),
+    "fold3": ((1, 3), (3, 2), (0, 1), (4, 2), (2, 3),),
+    "back3": ((0, 2), (3, 3), (1, 4), (0, 3), (2, 4),),
+    "relay3": ((3, 4), (0, 4), (4, 3), (4, 4),),
+}
 SCORE_SCALE = 0.125 * 1.4426950408889634
 
 
@@ -376,14 +404,23 @@
     norm_gains,
     head_gains,
     table_hbm,
+    block_out_hbm,
+    grad_in_hbm,
+    query_hbm,
+    key_hbm,
+    value_hbm,
+    wo_hbm,
+    out_norm_gains,
+    out_head_gains,
+    gate_hbm,
+    up_hbm,
+    down_hbm,
     block_out,
     grad_in,
     out_query,
     out_key,
     out_value,
     out_wo,
-    out_norm_gains,
-    out_head_gains,
     out_gate,
     out_up,
     out_down,
@@ -425,7 +462,6 @@
     part_b,
     landed,
     folded,
-    gain_pass,
     gain_got,
     g_send,
     g_recv,
@@ -436,15 +472,20 @@
     c_send,
     c_recv,
     l_sem,
+    o_sem,
 ):
     me = lax.axis_index("shard")
     ctx = lax.axis_index("ctx")
     chip, core = tp_place()
     own = pl.ds(pl.multiple_of(me * SHARD_ROWS, SHARD_ROWS), SHARD_ROWS)
     ctx_peer = {"ctx": 1 - ctx}
-    core_peer = {"tp": chip * 2 + 1 - core}
-    chip_peer = {"tp": (1 - chip) * 2 + core}
-    later = ctx.astype(F32)
+    group = [
+        {"ctx": lax.rem(ctx + k // 4, 2), "tp": lax.rem(chip * 2 + core + k % 4, 4)} for k in range(1, 8)
+    ]
+    partners = torus_partners() + group
+    barrier = pltpu.get_barrier_semaphore()
+    for partner in partners:
+        pl.semaphore_signal(barrier, inc=1, device_id=partner, device_id_type=MESH)
 
     def weight_copy(k, src, at, count, start=0):
         src = src.at[:, start : start + count]
@@ -454,7 +495,7 @@
         weight_copy(0, wq, 0, 256),
         weight_copy(1, wk, 256, 128),
         weight_copy(2, wv, 384, 128),
-        weight_copy(3, wo, 512, 256),
+        weight_copy(3, wo, OUT, 256),
     ]
     tile_copies = [
         weight_copy(4 + 3 * t + k, src, ATTN + STRIDE * t + TILE * k, TILE, TILE * t)
@@ -478,13 +519,48 @@
     block = jnp.zeros((128, 64), F32)
     for k in range(4):
         block = jnp.where(row == k, gain_sums[k : k + 1, 0:64], block)
-    w[own, 768:896] = dot(eye, block.astype(LOW), 1, 1).astype(LOW)
-    greet(torus_partners() + [ctx_peer, core_peer, chip_peer])
+    w[own, GAINS:OUT] = dot(eye, block.astype(LOW), 1, 1).astype(LOW)
     gather = [Gather(w, chunk, g_send, g_recv, 40 * i) for i, chunk in enumerate(CHUNKS)]
-    scatter = [Scatter(grads, landing, chunk, s_send, s_recv, 40 * i) for i, chunk in enumerate(CHUNKS)]
+
+    def scatter_step(i, step):
+        part = scatter[i]
+        if step == 0:
+            for j in range(4):
+                part.first(j)
+        elif step == 1:
+            for j in range(4):
+                part.second(j)
+        elif step == 2:
+            for j in range(3):
+                part.third(j)
+            part.first(4)
+            part.third(3)
+        elif step == 3:
+            part.second(4)
+        else:
+            part.third(4)
+            swap_chunk(i).start()
+
+    def swap_chunk(i):
+        lo, hi = PARTS[i] if i else (0, GAINS)
+        return remote(
+            grads.at[own, lo:hi], other.at[:, lo:hi], c_send.at[4 + i], c_recv.at[4 + i], ctx_peer
+        )
+
+    def add_up(place):
+        for part, step in SUMS.get(place, ()):
+            scatter_step(part, step)
+
+    def poll(place):
+        for chunk, step in POLLS.get(place, ()):
+            gather[chunk].step(step)
+
+    scatter = [Scatter(grads, landing, part, s_send, s_recv, 40 * i) for i, part in enumerate(PARTS)]
     for copy in first_copies:
         copy.wait()
+    pl.semaphore_wait(barrier, len(partners))
     gather[0].step(0)
+    gather[0].step(1)
 
     head_mean[...] = jnp.where(
         (iota((384, 384), 0) // 64) == (iota((384, 384), 1) // 64), 1.0 / 64, 0.0
@@ -495,30 +571,26 @@
     ).astype(LOW)
     gain_sums[...] = jnp.zeros_like(gain_sums)
     kv[:, 256:384] = jnp.ones((2 * TOKENS, 128), LOW)
-    for copy in tile_copies + token_copies:
-        copy.wait()
-    gather[0].step(1)
 
     def input_scale(i):
         x = hidden[row_block(i), :].astype(F32)
         inv_in[row_block(i), :] = lax.rsqrt(jnp.mean(x * x, axis=1, keepdims=True) + EPS)
 
+    token_copies[0].wait()
     loop(2, input_scale)
-    gather[0].step(2)
-    gather[1].step(0)
-    gather[0].step(3)
-    gather[0].step(4)
-    gather[0].step(5)
-    gather[2].step(0)
-    gather[1].step(1)
+    for copy in tile_copies:
+        copy.wait()
+    poll("scale")
 
     pick = (iota((16, 128), 0) == iota((16, 128), 1)).astype(F32).astype(LOW)
-    gain_rows[...] = dot(pick, w[:, 768:896], 1, 1)
+    gain_rows[...] = dot(pick, w[:, GAINS:OUT], 1, 1)
     head_rows = dot(gain_rows[...].astype(LOW), spread[...])
     head_gain[...] = jnp.concatenate([head_rows[2:3], head_rows[2:3], head_rows[3:4]], axis=1)
 
     def angles(rows):
         return wide(table[rows, 0:128]), wide(table[rows, 128:256])
+
+    token_copies[2].wait()
 
     def project(i):
         rows = row_block(i)
@@ -540,17 +612,27 @@
         kv[mine, 0:128] = turned[:, 256:384].astype(LOW)
         kv[mine, 128:256] = raw[:, 384:512].astype(LOW)
 
-    loop(2, project)
-    kv_copy = remote(
-        kv.at[TOKENS : 2 * TOKENS, 0:256],
-        kv.at[0:TOKENS, 0:256],
-        c_send.at[0],
-        c_recv.at[0],
-        ctx_peer,
-    )
-    kv_copy.start()
-    gather[1].step(2)
-    gather[3].step(0)
+    project(0)
+    poll("project")
+    project(1)
+    def kv_copy(i):
+        lanes = slice(128 * i, 128 * (i + 1))
+        return remote(
+            kv.at[TOKENS : 2 * TOKENS, lanes], kv.at[0:TOKENS, lanes], c_send.at[i], c_recv.at[i], ctx_peer
+        )
+
+    def kv_return(i):
+        lanes = slice(128 * i, 128 * (i + 1))
+        return remote(
+            kv_send.at[:, lanes], kv_got.at[:, lanes], c_send.at[2 + i], c_recv.at[2 + i], ctx_peer
+        )
+
+    @pl.when(ctx == 0)
+    def _():
+        for i in range(2):
+            kv_copy(i).start()
+        kv[0:TOKENS, 0:256] = jnp.zeros((TOKENS, 256), LOW)
+
 
     def attend_own(h):
         for i in range(2):
@@ -566,25 +648,43 @@
         for i in range(2):
             rows, keys = slice(ROWS * i, ROWS * (i + 1)), slice(0, TOKENS)
             scores = dot(q_heads[h, rows, :], kv[keys, 0:128], 1, 1)
-            weights = (jnp.exp2(scores * SCORE_SCALE) * later).astype(LOW)
+            weights = jnp.exp2(scores * SCORE_SCALE).astype(LOW)
             probs[h, rows, keys] = weights
             o_heads[h, rows, :] += dot(weights, kv[keys, 128:384])
 
-    loop(4, attend_own)
-    gather[1].step(3)
-    gather[2].step(1)
-    kv_copy.wait()
-    loop(4, attend_other)
-    gather[1].step(4)
-    gather[2].step(2)
+    poll("keys")
+    for h in range(4):
+        attend_own(h)
+        poll(f"own{h}")
+
+    @pl.when(ctx == 1)
+    def _():
+        kv_copy(0).wait_recv()
+        kv_copy(1).wait_recv()
+        loop(2, attend_other)
+
+    poll("other")
+
+    @pl.when(ctx == 1)
+    def _():
+        loop(2, lambda h: attend_other(h + 2))
+
+    poll("attended")
 
     sums = [
-        TpSum(part, landed.at[k], folded.at[k % 2], out, t_send, t_recv, 6 * k)
+        [
+            TpSum(half, part, landed.at[k, half], folded.at[k % 2, half], out, t_send, t_recv, 12 * k + 6 * half)
+            for half in range(2)
+        ]
         for k, (part, out) in enumerate(
             ((part_a, mlp_in), (part_b, d_branch), (part_a, block_out), (part_b, grad_in))
         )
     ]
-    mine = sums[0].mine
+
+    def each(k, *actions):
+        for action in actions:
+            for half in sums[k]:
+                getattr(half, action)()
 
     def attended_rows(i):
         rows = row_block(i, 128)
@@ -597,32 +697,38 @@
         )
         att[rows, :] = heads
         attended[rows, :] = heads.astype(LOW)
-        part_a[rows, :] = dot(heads.astype(LOW), w[:, 512:768], 1, 1).astype(LOW)
+        part_a[rows, :] = dot(heads.astype(LOW), w[:, OUT:ATTN], 1, 1).astype(LOW)
 
     loop(4, attended_rows)
-    sums[0].begin()
-    gather[1].step(5)
-    sums[0].fold()
-    gather[2].step(3)
-    gather[3].step(1)
-    residual = hidden[mine, :].astype(F32) + sums[0].total()
-    res_scale = lax.rsqrt(jnp.mean(residual * residual, axis=1, keepdims=True) + EPS)
-    res_own[...] = residual
-    mlp_in[mine, :] = (residual * res_scale * gain_rows[1:2, :]).astype(LOW)
-    sums[0].back()
-    gather[2].step(4)
-    gather[3].step(2)
-    sums[0].relay()
-    gather[3].step(3)
-    sums[0].end()
-
+    each(0, "begin")
+    poll("begin")
+    each(0, "fold")
+    poll("fold")
+    for half in sums[0]:
+        residual = hidden[half.mine, :].astype(F32) + half.total()
+        res_scale = lax.rsqrt(jnp.mean(residual * residual, axis=1, keepdims=True) + EPS)
+        res_own[half.local, :] = residual
+        mlp_in[half.mine, :] = (residual * res_scale * gain_rows[1:2, :]).astype(LOW)
+        half.back()
+    poll("back")
+    each(0, "relay")
+    poll("relay")
+    each(0, "end")
+
+    def weight_grads(t):
+        at = ATTN + STRIDE * t
+
+        def rows_of(n):
+            rows = row_block(n)
+            grads[rows, at : at + 2 * TILE] = dot(mlp_in[:, rows], dgu[t], 0, 0).astype(LOW)
+            grads[rows, at + 2 * TILE : at + 3 * TILE] = dot(cot[:, rows], hid[t], 0, 0).astype(LOW)
+
+        loop(4, rows_of)
+
+    token_copies[1].wait()
     for t in range(TILES):
         at = ATTN + STRIDE * t
-        if t == 1:
-            gather[2].step(5)
-            gather[3].step(4)
-        if t == 2:
-            gather[3].step(5)
+        poll(f"tile{t}")
 
         def feed(i):
             rows = row_block(i)
@@ -656,49 +762,41 @@
             total = term if total is None else total + term
         part_a[:, rows] = total.astype(LOW)
 
-    def weight_grads(t):
-        at = ATTN + STRIDE * t
-
-        def rows_of(n):
-            rows = row_block(n)
-            grads[rows, at : at + 2 * TILE] = dot(mlp_in[:, rows], dgu[t], 0, 0).astype(LOW)
-            grads[rows, at + 2 * TILE : at + 3 * TILE] = dot(cot[:, rows], hid[t], 0, 0).astype(LOW)
-
-        loop(4, rows_of)
-        for j in range(4):
-            scatter[t + 1].first(j)
-
     loop(4, mlp_back)
-    sums[1].begin()
+    each(1, "begin")
     weight_grads(0)
-    sums[1].fold()
+    add_up("begin1")
+    each(1, "fold")
+    weight_grads(1)
+    add_up("fold1")
+    weight_grads(2)
+    add_up("grads")
+    gain_mlp = jnp.zeros((1, WIDTH), F32)
+    for half in sums[1]:
+        residual = res_own[half.local, :]
+        res_scale = lax.rsqrt(jnp.mean(residual * residual, axis=1, keepdims=True) + EPS)
+        unit = residual * res_scale
+        d_mlp_in = half.total()
+        gain_mlp += jnp.sum(d_mlp_in * unit, axis=0, keepdims=True)
+        d_unit = d_mlp_in * gain_rows[1:2, :]
+        d_res = cot[half.mine, :].astype(F32) + res_scale * (
+            d_unit - unit * jnp.mean(d_unit * unit, axis=1, keepdims=True)
+        )
+        d_res_own[half.local, :] = d_res
+        d_branch[half.mine, :] = d_res.astype(LOW)
+        half.back()
+    gain_sums[1:2, :] = gain_mlp
     loop(4, mlp_out)
-    sums[2].begin()
-    weight_grads(1)
-    residual = res_own[...]
-    res_scale = lax.rsqrt(jnp.mean(residual * residual, axis=1, keepdims=True) + EPS)
-    unit = residual * res_scale
-    d_mlp_in = sums[1].total()
-    gain_sums[1:2, :] = jnp.sum(d_mlp_in * unit, axis=0, keepdims=True)
-    d_unit = d_mlp_in * gain_rows[1:2, :]
-    d_res = cot[mine, :].astype(F32) + res_scale * (
-        d_unit - unit * jnp.mean(d_unit * unit, axis=1, keepdims=True)
-    )
-    d_res_own[...] = d_res
-    d_branch[mine, :] = d_res.astype(LOW)
-    sums[1].back()
-    sums[2].fold()
-    weight_grads(2)
-    sums[1].relay()
-    for j in range(4):
-        scatter[1].second(j)
-    sums[1].end()
-    block_out[mine, :] = (res_own[...] + sums[2].total()).astype(LOW)
-    sums[2].back()
+    each(2, "begin")
+    add_up("back1")
+    each(1, "relay")
+    each(1, "end")
+    each(2, "fold")
+    add_up("end1")
 
     def attended_back(i):
         rows = row_block(i)
-        d_att = dot(d_branch[rows, :], w[:, 512:768]).astype(LOW).astype(F32)
+        d_att = dot(d_branch[rows, :], w[:, OUT:ATTN]).astype(LOW).astype(F32)
         scaled = (d_att * inverse[rows, :]).astype(LOW).astype(F32)
         delta = -split_dot(scaled * att[rows, :], head_mean[0:256, 0:256])
         first = iota((ROWS, 128), 1) < 64
@@ -713,6 +811,13 @@
             ).astype(LOW)
 
     loop(2, attended_back)
+
+    def out_grads(n):
+        rows = row_block(n)
+        grads[rows, OUT:ATTN] = dot(d_branch[:, rows], attended[...], 0, 0).astype(LOW)
+
+    loop(4, out_grads)
+    add_up("outgrads")
     kv_grad[...] = jnp.zeros_like(kv_grad)
 
     def back_piece(h, rows, keys):
@@ -733,28 +838,36 @@
             rows = slice(ROWS * i, ROWS * (i + 1))
             o_heads[h, rows, 0:128] += back_piece(h, rows, slice(TOKENS, TOKENS + ROWS * (i + 1)))
 
-    loop(4, back_other)
-    kv_send[:, 0:128] = (kv_grad[0:TOKENS, 0:128] * 0.125).astype(LOW)
-    kv_send[:, 128:256] = kv_grad[0:TOKENS, 128:256].astype(LOW)
-    kv_back = remote(kv_send, kv_got, c_send.at[1], c_recv.at[1], ctx_peer)
-    kv_back.start()
-    sums[2].relay()
-    for j in range(4):
-        scatter[2].second(j)
-    for j in range(3):
-        scatter[1].third(j)
-    scatter[1].first(4)
-    scatter[1].third(3)
-    loop(4, back_own)
-    for j in range(4):
-        scatter[3].second(j)
-    for j in range(3):
-        scatter[2].third(j)
-    scatter[2].first(4)
-    scatter[2].third(3)
-    scatter[1].second(4)
-    sums[2].end()
-    kv_back.wait()
+    @pl.when(ctx == 1)
+    def _():
+        loop(4, back_other)
+        kv_send[:, 0:128] = (kv_grad[0:TOKENS, 0:128] * 0.125).astype(LOW)
+        kv_send[:, 128:256] = kv_grad[0:TOKENS, 128:256].astype(LOW)
+        for i in range(2):
+            kv_return(i).start()
+
+    @pl.when(ctx == 0)
+    def _():
+        o_heads[:, :, 0:128] = jnp.zeros((4, TOKENS, 128), F32)
+
+    add_up("other")
+    loop(2, back_own)
+    add_up("own1")
+    loop(2, lambda h: back_own(h + 2))
+    add_up("own3")
+    for half in sums[2]:
+        block_out[half.mine, :] = (res_own[half.local, :] + half.total()).astype(LOW)
+        half.back()
+    add_up("block")
+
+    @pl.when(ctx == 0)
+    def _():
+        for i in range(2):
+            kv_return(i).wait_recv()
+
+    @pl.when(ctx == 1)
+    def _():
+        kv_got[...] = jnp.zeros_like(kv_got)
 
     def raw_back(i):
         rows = row_block(i)
@@ -782,12 +895,11 @@
         part_b[rows, :] = d_normed.astype(LOW)
 
     loop(2, normed_back)
-    sums[3].begin()
+    each(3, "begin")
 
     def attention_grads(n):
         rows = row_block(n)
         grads[rows, 0:512] = dot(normed[:, rows], d_raw[...], 0, 0).astype(LOW)
-        grads[rows, 512:768] = dot(d_branch[:, rows], attended[...], 0, 0).astype(LOW)
 
     loop(4, attention_grads)
     heads = gain_sums[4:5, 0:384]
@@ -803,66 +915,49 @@
         gain_sums[0:1, :],
         jnp.where(row == 1, gain_sums[1:2, :], dot(head_sums.astype(LOW), spread[...], 1, 1)),
     )
-    grads[:, 768:896] = dot(gain_all.astype(LOW), pick, 0, 0).astype(LOW)
-    for j in range(4):
-        scatter[0].first(j)
-    sums[3].fold()
-
-    def swap_chunk(i):
-        lo, hi = CHUNKS[i] if i else (0, 768)
+    grads[:, GAINS:OUT] = dot(gain_all.astype(LOW), pick, 0, 0).astype(LOW)
+    scatter_step(0, 0)
+    each(3, "fold")
+    add_up("fold3")
+    each(2, "relay")
+    for half in sums[3]:
+        rows = half.mine
+        d_normed = half.total()
+        unit = hidden[rows, :].astype(F32) * inv_in[rows, :]
+        d_unit = d_normed * gain_rows[0:1, :]
+        grad_in[rows, :] = (
+            d_res_own[half.local, :]
+            + inv_in[rows, :] * (d_unit - unit * jnp.mean(d_unit * unit, axis=1, keepdims=True))
+        ).astype(LOW)
+        half.back()
+    add_up("back3")
+    each(3, "relay")
+    add_up("relay3")
+
+    place = ctx * 4 + chip * 2 + core
+    gain_got[place] = grads[own, GAINS:OUT]
+
+    def gain_copy(k):
         return remote(
-            grads.at[own, lo:hi], other.at[:, lo:hi], c_send.at[2 + i], c_recv.at[2 + i], ctx_peer
+            grads.at[own, GAINS:OUT],
+            gain_got.at[place],
+            c_send.at[8 + k],
+            c_recv.at[8 + k],
+            group[k - 1],
         )
 
-    for j in range(3):
-        scatter[3].third(j)
-    scatter[3].first(4)
-    scatter[3].third(3)
-    scatter[1].third(4)
-    swap_chunk(1).start()
-    scatter[2].second(4)
-    for j in range(4):
-        scatter[0].second(j)
-    d_normed = sums[3].total()
-    unit = hidden[mine, :].astype(F32) * inv_in[mine, :]
-    d_unit = d_normed * gain_rows[0:1, :]
-    grad_in[mine, :] = (
-        d_res_own[...]
-        + inv_in[mine, :] * (d_unit - unit * jnp.mean(d_unit * unit, axis=1, keepdims=True))
-    ).astype(LOW)
-    sums[3].back()
-    for j in range(3):
-        scatter[0].third(j)
-    scatter[0].first(4)
-    scatter[0].third(3)
-    scatter[2].third(4)
-    swap_chunk(2).start()
-    scatter[3].second(4)
-    scatter[0].second(4)
-    sums[3].relay()
-    scatter[3].third(4)
-    swap_chunk(3).start()
-    scatter[0].third(4)
-    swap_chunk(0).start()
-
-    def gain_copy(k, src, target):
-        return remote(src, gain_got.at[k], c_send.at[6 + k], c_recv.at[6 + k], target)
-
-    gain_pass[0] = grads[own, 768:896]
-    passes = [
-        gain_copy(k, gain_pass.at[k], target)
-        for k, target in enumerate((core_peer, chip_peer, ctx_peer))
-    ]
-    for k in range(3):
-        passes[k].start()
-        passes[k].wait()
-        if k < 2:
-            total = gain_pass[k].astype(F32) + gain_got[k].astype(F32)
-            gain_pass[k + 1] = total.astype(LOW)
-        else:
-            turned = dot(pick, gain_pass[k], 1, 1) + dot(pick, gain_got[k], 1, 1)
-            out_norm_gains[...] = turned[0:2, :]
-            out_head_gains[...] = turned[2:4, 0:4]
+    for k in range(1, 8):
+        gain_copy(k).start()
+
+    written = []
+
+    def write(source, target):
+        copy = pltpu.make_async_copy(source, target, o_sem.at[len(written)])
+        copy.start()
+        written.append(copy)
+
+    each(2, "end")
+    write(block_out, block_out_hbm)
 
     def both_sums(lo, hi):
         return grads[own, lo:hi].astype(F32) + other[:, lo:hi].astype(F32)
@@ -873,16 +968,73 @@
         out_gate[:, lanes] = both_sums(at, at + TILE)
         out_up[:, lanes] = both_sums(at + TILE, at + 2 * TILE)
         out_down[:, lanes] = both_sums(at + 2 * TILE, at + 3 * TILE)
+        for source, target in ((out_gate, gate_hbm), (out_up, up_hbm), (out_down, down_hbm)):
+            write(source.at[:, lanes], target.at[:, lanes])
+    swap_chunk(4).wait()
+    out_wo[...] = both_sums(OUT, ATTN)
+    write(out_wo, wo_hbm)
+    each(3, "end")
+    write(grad_in, grad_in_hbm)
     swap_chunk(0).wait()
     out_query[...] = both_sums(0, 256)
     out_key[...] = both_sums(256, 384)
     out_value[...] = both_sums(384, 512)
-    out_wo[...] = both_sums(512, 768)
-    sums[3].end()
+    write(out_query, query_hbm)
+    write(out_key, key_hbm)
+    write(out_value, value_hbm)
+    turned = jnp.zeros((16, SHARD_ROWS), F32)
+    for k in range(1, 8):
+        gain_copy(k).wait()
+    for k in range(8):
+        turned = turned + dot(pick, gain_got[k], 1, 1)
+    out_norm_gains[...] = turned[0:2, :]
+    out_head_gains[...] = turned[2:4, 0:4]
+
+    @pl.when(ctx == 0)
+    def _():
+        for i in range(2):
+            kv_copy(i).wait_send()
+
+    @pl.when(ctx == 1)
+    def _():
+        for i in range(2):
+            kv_return(i).wait_send()
+
     for chunk in gather:
         chunk.finish()
     for chunk in scatter:
         chunk.finish()
+    for copy in written:
+        copy.wait()
+
+
+def finish_kernel(norm_in, head_in, grad_low, *refs):
+    sources, refs = refs[:8], refs[8:]
+    norm_out, head_out, grad_out, targets, refs = refs[0], refs[1], refs[2], refs[3:11], refs[11:]
+    low, full, held, refs = refs[0], refs[1], refs[2:10], refs[10:]
+    load_sem, store_sem, low_sem, full_sem = refs
+    pieces = [slice(128 * i, 128 * (i + 1)) for i in range(4)]
+    grad_loads = [
+        pltpu.make_async_copy(grad_low.at[p], low.at[p], low_sem.at[i]) for i, p in enumerate(pieces)
+    ]
+    grad_stores = [
+        pltpu.make_async_copy(full.at[p], grad_out.at[p], full_sem.at[i]) for i, p in enumerate(pieces)
+    ]
+    loads = [pltpu.make_async_copy(a, b, load_sem.at[i]) for i, (a, b) in enumerate(zip(sources, held))]
+    stores = [pltpu.make_async_copy(a, b, store_sem.at[i]) for i, (a, b) in enumerate(zip(held, targets))]
+    for copy in grad_loads + loads:
+        copy.start()
+    norm_out[...] = norm_in[...]
+    head_out[...] = head_in[...]
+    for piece, load, store in zip(pieces, grad_loads, grad_stores):
+        load.wait()
+        full[piece, :] = low[piece, :].astype(F32)
+        store.start()
+    for load, store in zip(loads, stores):
+        load.wait()
+        store.start()
+    for copy in stores + grad_stores:
+        copy.wait()
 
 
 def rotation_tables():
@@ -925,6 +1077,8 @@
         out((SHARD_ROWS, TILE * TILES), F32),
     ]
     scratch = [
+        pltpu.VMEM(value.shape, value.dtype) for k, value in enumerate(outs) if k not in (6, 7)
+    ] + [
         pltpu.VMEM((TOKENS, WIDTH), LOW),
         pltpu.VMEM((TOKENS, WIDTH), LOW),
         pltpu.VMEM((TOKENS, 256), F32),
@@ -961,19 +1115,19 @@
         pltpu.VMEM((WIDTH, 128), LOW),
         pltpu.VMEM((TOKENS, WIDTH), LOW),
         pltpu.VMEM((TOKENS, WIDTH), LOW),
-        pltpu.VMEM((4, 3, TOKENS // 4, WIDTH), LOW),
-        pltpu.VMEM((2, TOKENS // 4, WIDTH), LOW),
-        pltpu.VMEM((3, SHARD_ROWS, 128), LOW),
-        pltpu.VMEM((3, SHARD_ROWS, 128), LOW),
-        pltpu.SemaphoreType.DMA((160,)),
-        pltpu.SemaphoreType.DMA((160,)),
-        pltpu.SemaphoreType.DMA((160,)),
-        pltpu.SemaphoreType.DMA((160,)),
-        pltpu.SemaphoreType.DMA((24,)),
-        pltpu.SemaphoreType.DMA((24,)),
-        pltpu.SemaphoreType.DMA((9,)),
-        pltpu.SemaphoreType.DMA((9,)),
+        pltpu.VMEM((4, 2, 3, SHARE, WIDTH), LOW),
+        pltpu.VMEM((2, 2, SHARE, WIDTH), LOW),
+        pltpu.VMEM((8, SHARD_ROWS, 128), LOW),
+        pltpu.SemaphoreType.DMA((200,)),
+        pltpu.SemaphoreType.DMA((200,)),
+        pltpu.SemaphoreType.DMA((200,)),
+        pltpu.SemaphoreType.DMA((200,)),
+        pltpu.SemaphoreType.DMA((48,)),
+        pltpu.SemaphoreType.DMA((48,)),
         pltpu.SemaphoreType.DMA((16,)),
+        pltpu.SemaphoreType.DMA((16,)),
+        pltpu.SemaphoreType.DMA((16,)),
+        pltpu.SemaphoreType.DMA((15,)),
     ]
     (
         block_out,
@@ -991,7 +1145,7 @@
         block_kernel,
         out_shape=outs,
         in_specs=[hbm] * 9 + [vmem] * 2 + [hbm],
-        out_specs=[vmem] * 11,
+        out_specs=[hbm] * 6 + [vmem] * 2 + [hbm] * 3,
         scratch_shapes=scratch,
         compiler_params=pltpu.CompilerParams(
             collective_id=0, has_side_effects=True, vmem_limit_bytes=VMEM_LIMIT
@@ -1011,9 +1165,35 @@
         head_gains,
         rotation_tables(),
     )
+    plain = [block_out, r_query, r_key, r_value, r_out, r_gate, r_up, r_down]
+    r_norm_gains, r_head_gains, grad_in, block_out, r_query, r_key, r_value, r_out, r_gate, r_up, r_down = (
+        pl.pallas_call(
+            finish_kernel,
+            out_shape=[
+                out(r_norm_gains.shape, F32),
+                out(r_head_gains.shape, F32),
+                out(grad_in.shape, F32),
+            ]
+            + [out(value.shape, value.dtype) for value in plain],
+            in_specs=[vmem] * 2 + [hbm] * 9,
+            out_specs=[vmem] * 2 + [hbm] * 9,
+            scratch_shapes=[
+                pltpu.VMEM((TOKENS, WIDTH), LOW),
+                pltpu.VMEM((TOKENS, WIDTH), F32),
+            ]
+            + [pltpu.VMEM(value.shape, value.dtype) for value in plain]
+            + [
+                pltpu.SemaphoreType.DMA((8,)),
+                pltpu.SemaphoreType.DMA((8,)),
+                pltpu.SemaphoreType.DMA((4,)),
+                pltpu.SemaphoreType.DMA((4,)),
+            ],
+            name="write_results",
+        )(r_norm_gains, r_head_gains, grad_in, *plain)
+    )
     return (
         block_out[None],
-        grad_in.astype(F32)[None],
+        grad_in[None],
         r_query,
         r_key,
         r_value,

time: 162 us -> 146 us (0.901)
  local copies, waits for them, and re-layouts: 6.77 us -> 0 us
  Pallas kernels: 150 us -> 145 us
  other arithmetic: 2.89 us -> 0 us
    pallas_call x1, Pallas kernels: 150 us -> 140 us  [per_device(): pl.pallas_call(block_kernel, out_shape=outs, in_specs=[hbm] * 9 + [vmem]...]
    unnamed x30 -> x0, local copies, waits for them, and re-layouts: 6.77 us -> none
    pallas_call x0 -> x1, Pallas kernels: none -> 4.84 us  [per_device(): pl.pallas_call(finish_kernel, out_shape=[out(r_norm_gains.shape, F32), ou...]
    broadcast_in_dim x1 -> x0, other arithmetic: 2.89 us -> none  [per_device(): grad_in.astype(F32)[None]]
where the time goes in v1:
time: 146 us
  Pallas kernels  145 us (99%)
    pallas_call x1, Pallas kernels, per_device(): pl.pallas_call(block_kernel, out_shape=outs, in_specs=[hbm] * 9 + [vmem]...  140 us
    pallas_call x1, Pallas kernels, per_device(): pl.pallas_call(finish_kernel, out_shape=[out(r_norm_gains.shape, F32), ou...  4.84 us

profile of v1, /device:TPU:1, one launch (start us, length us, event | category | flops | bytes accessed | tf_op | source)
XLA Modules:
  0.0 146.0 jit_solution(4232233894322437309)
XLA Ops:
  0.6 140.4 %transformer_block.1 = (bf16[512,1024]{1,0:T(8,128)(2,1)}, bf16[512,1024]{1,0:T(8,128)(2,1)}, f32[64,256]{1,0:T(8,128)}, f32[64,128]{1,0:T(8,128)}, f32[64,128]{...) custom-call(bf16[512,1024]{1,0:T(8,128)(2,1)} %bitcast.8, ...), custom_call_target="tpu_custom_call" | custom-call | tf_op jit(solution)/shard_map/transformer_block/pallas_call | solution.py:1144
  141.0 4.8 %write_results.1 = (f32[2,64]{1,0:T(2,128)}, f32[2,4]{1,0:T(2,128)}, f32[512,1024]{1,0:T(8,128)}, bf16[512,1024]{1,0:T(8,128)(2,1)}, f32[64,256]{1,0:T(8,128)}, ...) custom-call(f32[2,64]{1,0:T(2,128)} %get-tuple-element.33.norm_in, ...), custom_call_target="tpu_custom_call" | custom-call | tf_op jit(solution)/shard_map/write_results/pallas_call | solution.py:1170

commit v2 on v1

--- a/solution.py
+++ b/solution.py
@@ -314,7 +314,7 @@
     "tile2": ((3, 5),),
 }
 SUMS = {
-    "begin1": ((1, 0),),
+    "tile1": ((1, 0),),
     "fold1": ((2, 0),),
     "grads": ((3, 0),),
     "back1": ((1, 1),),
@@ -743,6 +743,9 @@
             dgu[t, rows, TILE : 2 * TILE] = (d_hidden * silu).astype(LOW)
 
         loop(2, feed)
+        if t == 1:
+            weight_grads(0)
+            add_up("tile1")
 
     def mlp_back(n):
         rows = row_block(n)
@@ -764,8 +767,6 @@
 
     loop(4, mlp_back)
     each(1, "begin")
-    weight_grads(0)
-    add_up("begin1")
     each(1, "fold")
     weight_grads(1)
     add_up("fold1")

time: 146 us -> 145 us (level)
  no operation moved by 1% of the time
where the time goes in v2:
time: 145 us
  Pallas kernels  144 us (99%)
    pallas_call x1, Pallas kernels, per_device(): pl.pallas_call(block_kernel, out_shape=outs, in_specs=[hbm] * 9 + [vmem]...  140 us
    pallas_call x1, Pallas kernels, per_device(): pl.pallas_call(finish_kernel, out_shape=[out(r_norm_gains.shape, F32), ou...  4.84 us

profile of v2, /device:TPU:1, one launch (start us, length us, event | category | flops | bytes accessed | tf_op | source)
XLA Modules:
  0.0 145.3 jit_solution(15883767301220038381)
XLA Ops:
  0.6 139.6 %transformer_block.1 = (bf16[512,1024]{1,0:T(8,128)(2,1)}, bf16[512,1024]{1,0:T(8,128)(2,1)}, f32[64,256]{1,0:T(8,128)}, f32[64,128]{1,0:T(8,128)}, f32[64,128]{...) custom-call(bf16[512,1024]{1,0:T(8,128)(2,1)} %bitcast.8, ...), custom_call_target="tpu_custom_call" | custom-call | tf_op jit(solution)/shard_map/transformer_block/pallas_call | solution.py:1145
  140.3 4.8 %write_results.1 = (f32[2,64]{1,0:T(2,128)}, f32[2,4]{1,0:T(2,128)}, f32[512,1024]{1,0:T(8,128)}, bf16[512,1024]{1,0:T(8,128)(2,1)}, f32[64,256]{1,0:T(8,128)}, ...) custom-call(f32[2,64]{1,0:T(2,128)} %get-tuple-element.33.norm_in, ...), custom_call_target="tpu_custom_call" | custom-call | tf_op jit(solution)/shard_map/write_results/pallas_call | solution.py:1171
